TPU v7x, 32 devices: a whole 2x2x4 slice. The times are simulated.
32 devices in a mesh: groups: 2 (over x), ctx: 16 (over z, y, core).
Axes of the slice: x: 2, y: 2, z: 4, core: 2. Of those that a mesh axis runs over, the one named last changes fastest.
Arguments:
- ttt_query: bfloat16 [4096, 2048], P(('groups', 'ctx')), parts along dimension 0, may hold values from -6 to 6
- ttt_key: bfloat16 [4096, 2048], P(('groups', 'ctx')), parts along dimension 0, may hold values from -6 to 6
- ttt_value: bfloat16 [4096, 2048], P(('groups', 'ctx')), parts along dimension 0, may hold values from -6 to 6
- lr_logit: float32 [4096, 32], P(('groups', 'ctx')), parts along dimension 0, may hold values from -8 to 8
- lr_base: float32 [32], replicated, may hold values from 0.001953125 to 0.125
- init_weight: float32 [32, 64, 64], replicated, may hold values from -0.75 to 0.75
- attn_query: bfloat16 [4096, 2048], P(('groups', 'ctx')), parts along dimension 0, may hold values from -64 to 64
- attn_key: bfloat16 [4096, 2048], P(('groups', 'ctx')), parts along dimension 0, may hold values from -4 to 4
- attn_value: bfloat16 [4096, 2048], P(('groups', 'ctx')), parts along dimension 0, may hold values from -6 to 6
- gain_ttt: float32 [2048], replicated, may hold values from 0.5 to 1.5
- gain_attn: float32 [2048], replicated, may hold values from 0.5 to 1.5
Outputs:
- mixed: bfloat16 [4096, 2048], P(('groups', 'ctx')), parts along dimension 0
There are 2 independent parts, one for each index of `groups`. A program takes and returns all parts, laid end to end along the dimension named above; an argument that names none is the same for every part. Nothing has to cross between parts.
All inputs are finite; a program needn't handle non-finite values.
Results may differ from a plain program's by a relative error of at most 0.0036.
Values may be sent and summed in bfloat16 or wider, within the bound.
A program may use at most 320 MiB of HBM per device.

v0:
```python
import math

import jax
import jax.numpy as jnp
from jax import lax
from jax.sharding import PartitionSpec as P

HEADS = 32
HD = 64
MB = 16
WIN_BLOCKS = 2


def carried_in(value, axis, join, neutral):
    count, mine = (lax.axis_size(axis), lax.axis_index(axis))
    pieces = jax.tree.map(lambda part: lax.all_gather(part, axis), value)
    running = jax.tree.map(
        lambda part, zero: jnp.full_like(part, 0) + jnp.asarray(zero, part.dtype), value, neutral
    )

    def step(position, running):
        longer = join(running, jax.tree.map(lambda part: part[position], pieces))
        return jax.tree.map(lambda new, old: jnp.where(position < mine, new, old), longer, running)

    return lax.fori_loop(0, count - 1, step, running)


def from_behind(value, axis, steps):
    count = lax.axis_size(axis)
    first, last = (max(0, -steps), min(count, count - steps))
    return lax.ppermute(value, axis, [(source, source + steps) for source in range(first, last)])


def ttt_step(weight, item):
    query, keys, values, rates = item
    high = lax.Precision.HIGHEST
    grads = jnp.einsum("shd,hde->she", keys, weight, precision=high) - values
    base = jnp.einsum("shd,hde->she", query, weight, precision=high)
    inner = (
        jnp.einsum("thd,shd->hts", query, keys, precision=high) * jnp.transpose(rates)[:, None, :]
    )
    lower = jnp.arange(query.shape[0])[:, None] >= jnp.arange(query.shape[0])[None, :]
    inner = jnp.where(lower[None], inner, 0.0)
    output = base - jnp.einsum("hts,she->the", inner, grads, precision=high)
    weight = weight - jnp.einsum("shd,she->hde", keys * rates[..., None], grads, precision=high)
    return (weight, output)


def compose_step(total, item):
    keys, values, rates = item
    high = lax.Precision.HIGHEST
    linear, shift_part = total
    scaled = keys * rates[..., None]
    eye = jnp.eye(HD, dtype=jnp.float32)
    transition = eye[None] - jnp.einsum("shd,she->hde", scaled, keys, precision=high)
    offset = jnp.einsum("shd,she->hde", scaled, values, precision=high)
    new_linear = jnp.einsum("hde,hef->hdf", transition, linear, precision=high)
    new_shift = jnp.einsum("hde,hef->hdf", transition, shift_part, precision=high) + offset
    return ((new_linear, new_shift), None)


def combine_maps(earlier, later):
    high = lax.Precision.HIGHEST
    new_linear = jnp.einsum("hde,hef->hdf", later[0], earlier[0], precision=high)
    new_shift = jnp.einsum("hde,hef->hdf", later[0], earlier[1], precision=high) + later[1]
    return (new_linear, new_shift)


def window_attention(query, keys, values, valid_from):
    rows = query.shape[0]
    span = keys.shape[0]
    group = min(8, HEADS)
    q_three = query.reshape(rows, HEADS, HD)
    k_three = keys.reshape(span, HEADS, HD)
    v_three = values.reshape(span, HEADS, HD)
    offset = (
        jnp.arange(rows, dtype=jnp.int32)[:, None]
        - jnp.arange(span, dtype=jnp.int32)[None, :]
        + (span - rows)
    )
    column = jnp.arange(span, dtype=jnp.int32)[None, :]
    allowed = (offset >= 0) & (offset < span - rows) & (column >= valid_from)
    pieces = []
    for start in range(0, HEADS, group):
        q_group = q_three[:, start : start + group, :]
        k_group = k_three[:, start : start + group, :]
        v_group = v_three[:, start : start + group, :]
        scores = jnp.einsum(
            "qhd,khd->hqk", q_group, k_group, preferred_element_type=jnp.float32
        ) / math.sqrt(HD)
        scores = jnp.where(allowed[None], scores, -1e30)
        largest = jnp.max(scores, axis=-1, keepdims=True)
        expo = jnp.exp(scores - largest)
        totals = jnp.sum(expo, axis=-1)
        weights = expo.astype(jnp.bfloat16)
        mixed = jnp.einsum("hqk,khd->qhd", weights, v_group, preferred_element_type=jnp.float32)
        pieces.append(mixed / jnp.transpose(totals)[:, :, None])
    return jnp.concatenate(pieces, axis=1)


def normed(values):
    return values * lax.rsqrt(jnp.mean(values * values, axis=-1, keepdims=True) + 1e-05)


def per_device(
    ttt_query,
    ttt_key,
    ttt_value,
    lr_logit,
    lr_base,
    init_weight,
    attn_query,
    attn_key,
    attn_value,
    gain_ttt,
    gain_attn,
):
    rows = ttt_query.shape[0]
    count = rows // MB
    query = ttt_query.astype(jnp.float32).reshape(count, MB, HEADS, HD)
    keys = ttt_key.astype(jnp.float32).reshape(count, MB, HEADS, HD)
    keys = keys * lax.rsqrt(jnp.mean(keys * keys, axis=-1, keepdims=True) + 1e-06) / math.sqrt(HD)
    values = ttt_value.astype(jnp.float32).reshape(count, MB, HEADS, HD)
    rates = (lr_base[None, :] * jax.nn.sigmoid(lr_logit)).reshape(count, MB, HEADS)
    eye = jnp.broadcast_to(jnp.eye(HD, dtype=jnp.float32)[None], (HEADS, HD, HD))
    identity = (eye, jnp.zeros_like(eye))
    block_map, _ = lax.scan(compose_step, identity, (keys, values, rates))
    prefix = carried_in((block_map[0], block_map[1]), "ctx", combine_maps, identity)
    start_weight = (
        jnp.einsum("hde,hef->hdf", prefix[0], init_weight, precision=lax.Precision.HIGHEST)
        + prefix[1]
    )
    _, ttt_out = lax.scan(ttt_step, start_weight, (query, keys, values, rates))
    ttt_out = ttt_out.reshape(rows, HEADS, HD)
    paired = jnp.stack((attn_key, attn_value))
    blocks = [paired]
    current = paired
    for step in range(WIN_BLOCKS):
        current = from_behind(current, "ctx", 1)
        blocks.append(current)
    window = jnp.concatenate(blocks[::-1], axis=1)
    valid_from = (WIN_BLOCKS - lax.axis_index("ctx")) * rows
    attn_out = window_attention(attn_query, window[0], window[1], valid_from)
    first = normed(ttt_out).reshape(rows, HEADS * HD) * gain_ttt
    second = normed(attn_out).reshape(rows, HEADS * HD) * gain_attn
    return (0.5 * (first + second)).astype(jnp.bfloat16)


def solution(mesh):
    in_specs = (
        P(("groups", "ctx"), None),
        P(("groups", "ctx"), None),
        P(("groups", "ctx"), None),
        P(("groups", "ctx"), None),
        P(),
        P(),
        P(("groups", "ctx"), None),
        P(("groups", "ctx"), None),
        P(("groups", "ctx"), None),
        P(),
        P(),
    )
    out_specs = P(("groups", "ctx"), None)
    return jax.shard_map(
        per_device, mesh=mesh, in_specs=in_specs, out_specs=out_specs, check_vma=False
    )
```

profile of v0, /device:TPU:28, one launch (start us, length us, event | category | flops | bytes accessed | tf_op | source)
XLA Modules:
  0.0 558.7 jit_solution(10033093455453927029)
XLA Ops:
  18.4 92.5 %while.42 = (s32[]{:T(128)}, f32[32,64,64]{2,1,0:T(8,128)}, f32[32,64,64]{2,1,0:T(8,128)}, f32[8,16,32,64]{3,1,2,0:T(8,128)}, f32[8,16,32]{1,2,0:T(8,128)S(1)}, ...) while((s32[]{:T(128)}, f32[32,64,64]{2,1,0:T(8,128)}, f32[32,64,64]{2,1,0:T(8,128)}, ...), condition=%wide.region_2.3_spmd.clone, body=%wide.region_1.2_spmd.clone.sunk | while | flops 252125184 | bytes 10004607 | solution.py:127
  18.4 3.0 convolution_subtract_fusion.5
  21.4 3.0 fusion.144
  30.0 3.0 convolution_subtract_fusion.5
  41.5 3.0 convolution_subtract_fusion.5
  53.1 3.0 convolution_subtract_fusion.5
  64.7 3.0 convolution_subtract_fusion.5
  76.2 3.0 convolution_subtract_fusion.5
  87.8 3.0 convolution_subtract_fusion.5
  99.4 3.0 convolution_subtract_fusion.5
  114.2 25.5 %collective-permute-done = bf16[2,128,2048]{2,1,0:T(8,128)(2,1)} collective-permute-done((bf16[2,128,2048]{2,1,0:T(8,128)(2,1)S(1)}, bf16[2,128,2048]{2,1,0:T(8,128)(2,1)}, u32[]{:S(2)}, u32[]{:S(2)}) %collective-permute-start) | collective-permute-done | bytes 1048608 | tf_op jit(solution)/shard_map/ppermute | solution.py:31
  146.7 9.4 %collective-permute-done.1 = bf16[2,128,2048]{2,1,0:T(8,128)(2,1)} collective-permute-done((bf16[2,128,2048]{2,1,0:T(8,128)(2,1)}, bf16[2,128,2048]{2,1,0:T(8,128)(2,1)}, u32[]{:S(2)}, u32[]{:S(2)}) %collective-permute-start.1) | collective-permute-done | bytes 1048608 | tf_op jit(solution)/shard_map/ppermute | solution.py:31
  174.4 73.6 %all-gather.5.cloned.1.call-done = f32[512,64,64]{2,1,0:T(8,128)} async-done(((f32[32,64,64]{2,1,0:T(8,128)}), f32[512,64,64]{2,1,0:T(8,128)}) %all-gather.5.cloned.1.call-update) | async-done | bytes 8388624 | tf_op jit(solution)/shard_map/all_gather | solution.py:16
  248.0 127.3 %all-gather.7.cloned.1.call-done = f32[512,64,64]{2,1,0:T(8,128)} async-done(((f32[32,64,64]{2,1,0:T(8,128)}), f32[512,64,64]{2,1,0:T(8,128)}) %all-gather.7.cloned.1.call-update) | async-done | bytes 8388624 | tf_op jit(solution)/shard_map/all_gather | solution.py:16
  375.4 82.8 %while.43 = (s32[]{:T(128)}, f32[32,64,64]{2,1,0:T(8,128)S(1)}, f32[32,64,64]{2,1,0:T(8,128)S(1)}, s32[]{:T(128)}, f32[16,32,64,64]{3,2,1,0:T(8,128)}, /*index=5*/f32[16,32,64,64]{3,2,1,0:T(8,128)}, s32[]{:T(128)}, s32[]{:T(128)}) while((s32[]{:T(128)}, f32[32,64,64]{2,1,0:T(8,128)S(1)}, f32[32,64,64]{2,1,0:T(8,128)S(1)}, ...), condition=%wide.region_4.5_spmd.clone, body=%wide.region_3.4_spmd.clone.sunk | while | flops 201981952 | bytes 10488936 | solution.py:25
  461.6 79.4 %while.41 = (s32[]{:T(128)}, f32[32,64,64]{2,1,0:T(8,128)S(1)}, f32[8,16,32,64]{3,1,2,0:T(8,128)}, f32[8,16,32,64]{3,1,2,0:T(8,128)}, f32[8,16,32]{1,2,0:T(8,128...) while((s32[]{:T(128)}, f32[32,64,64]{2,1,0:T(8,128)S(1)}, ...), condition=%wide.region_6.7_spmd, body=%wide.region_5.6_spmd.sunk | while | flops 88326400 | bytes 4666461 | solution.py:133
  468.7 3.0 convolution_subtract_fusion.4
  478.7 3.0 convolution_subtract_fusion.4
  488.6 3.0 convolution_subtract_fusion.4
  498.5 3.0 convolution_subtract_fusion.4
  508.4 3.0 convolution_subtract_fusion.4
  518.3 3.0 convolution_subtract_fusion.4
  528.2 3.0 convolution_subtract_fusion.4
  538.0 3.0 convolution_subtract_fusion.4
  (272 shorter events, 257.1 us)
Async XLA Ops:
  6.5 452.7 %copy-start = (f32[32,64,64]{2,1,0:T(8,128)S(1)}, f32[32,64,64]{2,1,0:T(8,128)}, u32[]{:S(2)}) copy-start(f32[32,64,64]{2,1,0:T(8,128)} %param.22) | copy-start | bytes 1572868
  6.5 241.4 %all-gather.5.cloned.1.call-start = ((), (), s32[]{:S(2)}) async-start(), calls=%async_computation | async-start | bytes 17825792 | tf_op jit(solution)/shard_map/all_gather | solution.py:16
  14.4 2.6 copy-start.11
  14.4 2.6 copy-start.14
  25.6 2.2 copy-start.1
  37.1 2.2 copy-start.1
  48.7 2.2 copy-start.1
  60.3 2.2 copy-start.1
  71.8 2.2 copy-start.1
  83.4 2.2 copy-start.1
  95.0 2.2 copy-start.1
  106.5 2.2 copy-start.1
  110.9 1.2 copy-start.7
  111.0 264.3 %all-gather.7.cloned.1.call-start = ((), (), s32[]{:S(2)}) async-start(), calls=%async_computation.1 | async-start | bytes 17825792 | tf_op jit(solution)/shard_map/all_gather | solution.py:16
  112.2 27.5 %collective-permute-start = (bf16[2,128,2048]{2,1,0:T(8,128)(2,1)S(1)}, bf16[2,128,2048]{2,1,0:T(8,128)(2,1)}, u32[]{:S(2)}, u32[]{:S(2)}) collective-permute-start(bf16[2,128,2048]{2,1,0:T(8,128)(2,1)S(1)} %pad_maximum_fusion), channel_id=1, source_target_pairs={{0,1},{1,2},{2,3},{3,4},{4,5},{5,6},{6,7},{7,8},{8,9},{9,10},{10,1... | collective-permute-start | bytes 3145736 | tf_op jit(solution)/shard_map/ppermute | solution.py:31
  139.7 16.4 %collective-permute-start.1 = (bf16[2,128,2048]{2,1,0:T(8,128)(2,1)}, bf16[2,128,2048]{2,1,0:T(8,128)(2,1)}, u32[]{:S(2)}, u32[]{:S(2)}) collective-permute-start(bf16[2,128,2048]{2,1,0:T(8,128)(2,1)} %collective-permute-done), channel_id=1, source_target_pairs={{0,1},{1,2},{2,3},{3,4},{4,5},{5,6},{6,7},{7,8},{8,9},{9,10},{10,1... | collective-permute-start | bytes 3145736 | tf_op jit(solution)/shard_map/ppermute | solution.py:31
  162.4 2.6 copy-start.10
  166.5 1.4 copy-start.9
  169.8 1.4 copy-start.8
  541.0 2.4 copy-start.3
  545.9 3.7 copy-start.4
  545.9 3.7 copy-start.5
  545.9 3.7 copy-start.12
  545.9 3.7 copy-start.13
  (2 other events, 2.0 us)
Sparse Core Ops, SparseCore 0:
  111.1 136.8 all-gather.4
  250.1 125.0 all-gather.6
where the time goes:
time: 567 us; the launch traced here: 559 us
  matrix products  239 us (42%)
  waiting for transfers between devices  236 us (42%)
  local copies, waits for them, and re-layouts  56.4 us (10%)
  between operations  13.7 us (2%)
  other arithmetic  7.5 us (1%)
    all_gather x2, waiting for transfers between devices, carried_in(): pieces = jax.tree.map(lambda part: lax.all_gather(part, axis), value)  201 us
    dot_general x15, matrix products, combine_maps(): jnp.einsum('hde,hef->hdf', later[0], earlier[1], precision=high) + later[1]  42.9 us
    dot_general x15, matrix products, combine_maps(): jnp.einsum('hde,hef->hdf', later[0], earlier[0], precision=high)  36.6 us
    ppermute x2, waiting for transfers between devices, from_behind(): lax.ppermute(value, axis, [(source, source + steps) for source in range(f...  34.9 us
    dot_general x8, matrix products, ttt_step(): jnp.einsum('shd,she->hde', keys * rates[..., None], grads, precision=high)  23.9 us
    dot_general x8, matrix products, compose_step(): jnp.einsum('shd,she->hde', scaled, keys, precision=high)  23.7 us
    dot_general x8, matrix products, compose_step(): offset = jnp.einsum('shd,she->hde', scaled, values, precision=high)  23.6 us
    dot_general x8, matrix products, compose_step(): jnp.einsum('hde,hef->hdf', transition, shift_part, precision=high) + offset  17.3 us
  transfers between devices with their start and end apart: 4, of which 4 were waited for; matrix products, arithmetic and copies ran while one was open for 4% of the time, Pallas kernels for 0%

commit v1 on v0

v1 whole, which is shorter than its diff:
```python
import functools
import math

import jax
import jax.numpy as jnp
from jax import lax
from jax.experimental import pallas as pl
from jax.experimental.pallas import tpu as pltpu
from jax.sharding import PartitionSpec as P

HD = 64
MB = 16
PAIR = 2 * HD
CHUNK = 2
F32 = jnp.float32
BF16 = jnp.bfloat16


def mm(a, b):
    return jnp.dot(a, b, preferred_element_type=F32)


def mmt(a, b):
    return lax.dot_general(a, b, (((1,), (1,)), ((), ())), preferred_element_type=F32)


def split(x):
    high = x.astype(BF16)
    return high, (x - high.astype(F32)).astype(BF16)


def stack_right(high, low):
    top = jnp.concatenate([high, low], axis=1)
    bottom = jnp.concatenate([high, jnp.zeros_like(low)], axis=1)
    return jnp.concatenate([top, bottom], axis=0)


def fold(x):
    half = x.shape[1] // 2
    return x[:, :half] + x[:, half:]


def dot_split(a, right):
    return fold(mm(jnp.concatenate(split(a), axis=1), right))


def dot_full(a, b):
    return dot_split(a, stack_right(*split(b)))


def swap(x):
    return pltpu.roll(x, HD, 1)


def kernel(
    count,
    tq_ref,
    tk_ref,
    tv_ref,
    logit_ref,
    base_ref,
    init_ref,
    aq_ref,
    ak_ref,
    av_ref,
    gt_ref,
    ga_ref,
    out_ref,
    kbuf,
    vbuf,
    eta_ref,
    z_ref,
    b_ref,
    p_ref,
    r_ref,
    att_ref,
    win,
    wout,
    kv_send,
    kv_recv,
    w_send,
    w_recv,
):
    rows, width = tq_ref.shape
    pairs = width // PAIR
    chunks = pairs // CHUNK
    heads = width // HD
    me = lax.axis_index("ctx")

    barrier = pltpu.get_barrier_semaphore()
    for back in (1, 2):

        @pl.when(me >= back)
        def _():
            pl.semaphore_signal(
                barrier,
                inc=1,
                device_id={"ctx": me - back},
                device_id_type=pl.DeviceIdType.MESH,
            )

    @pl.when(me + 1 < count)
    def _():
        pl.semaphore_wait(barrier, jnp.minimum(count - 1 - me, 2))

    def kv_copy(ahead, which):
        source, target = ((ak_ref, kbuf), (av_ref, vbuf))[which]
        at = 2 * (ahead - 1) + which
        return pltpu.make_async_remote_copy(
            src_ref=source,
            dst_ref=target.at[2 - ahead],
            send_sem=kv_send.at[at],
            recv_sem=kv_recv.at[at],
            device_id={"ctx": me + ahead},
            device_id_type=pl.DeviceIdType.MESH,
        )

    for ahead in (1, 2):

        @pl.when(me + ahead < count)
        def _():
            for which in range(2):
                kv_copy(ahead, which).start()

        @pl.when(me < ahead)
        def _():
            kbuf[2 - ahead] = jnp.zeros((rows, width), BF16)
            vbuf[2 - ahead] = jnp.zeros((rows, width), BF16)

    def w_copy(chunk):
        span = pl.ds(chunk * CHUNK, CHUNK)
        return pltpu.make_async_remote_copy(
            src_ref=wout.at[span],
            dst_ref=win.at[span],
            send_sem=w_send.at[chunk],
            recv_sem=w_recv.at[chunk],
            device_id={"ctx": me + 1},
            device_id_type=pl.DeviceIdType.MESH,
        )

    @pl.when(me == 0)
    def _():
        @pl.loop(0, pairs)
        def _(p):
            win[p] = jnp.concatenate([init_ref[2 * p], init_ref[2 * p + 1]], axis=1)

    eta_ref[...] = base_ref[...] * jax.nn.sigmoid(logit_ref[...])

    row = lax.broadcasted_iota(jnp.int32, (rows, rows), 0)
    col = lax.broadcasted_iota(jnp.int32, (rows, rows), 1)
    lane = lax.broadcasted_iota(jnp.int32, (rows, PAIR), 1)
    head_lane = lax.broadcasted_iota(jnp.int32, (rows, heads), 1)
    first = lane < HD
    first_w = first[:HD]
    lower = row >= col

    def columns(p):
        return pl.ds(pl.multiple_of(p * PAIR, PAIR), PAIR)

    def keep(half, x):
        return jnp.where(first, x, 0.0) if half == 0 else jnp.where(first, 0.0, x)

    def head_sum(half, x):
        return jnp.sum(keep(half, x), axis=1, keepdims=True)

    @pl.loop(0, pairs // 2)
    def _(step):
        items = []
        for u in range(2):
            p = step * 2 + u
            cols = columns(p)
            kp, qp = tk_ref[:, cols], tq_ref[:, cols]
            kf, qf = kp.astype(F32), qp.astype(F32)
            vf = tv_ref[:, cols].astype(F32)
            kt = jnp.transpose(kf).astype(BF16)
            square = kf * kf
            for half in range(2):
                scale = lax.rsqrt(head_sum(half, square) * (1.0 / HD) + 1e-6) * (1.0 / math.sqrt(HD))
                eta = jnp.sum(
                    jnp.where(head_lane == 2 * p + half, eta_ref[...], 0.0), axis=1, keepdims=True
                )
                own = keep(half, kf).astype(BF16)
                near = scale * eta
                rate = near * scale
                gram = jnp.where((row // MB) > (col // MB), mmt(own, kp) * rate, 0.0)
                cross = jnp.where(lower, mmt(qp, own), 0.0)
                k_low = kf if half == 0 else swap(kf)
                q_low = qf if half == 0 else swap(qf)
                v_high = swap(vf) if half == 0 else vf
                right = jnp.where(first, rate * k_low, near * v_high)
                items.append([gram, cross, right, kt, q_low])
        size = MB
        inverse = [jnp.where(row == col, 1.0, 0.0)] * len(items)
        while size < rows:
            band = ((row // (2 * size)) == (col // (2 * size))) & ((row // size) != (col // size))
            parts = [jnp.where(band, item[0], 0.0) for item in items]
            if size == MB:
                inverse = [a - part for a, part in zip(inverse, parts)]
            else:
                rights = [stack_right(*split(a)) for a in inverse]
                parts = [dot_full(a, part) for a, part in zip(inverse, parts)]
                parts = [dot_split(part, r) for part, r in zip(parts, rights)]
                inverse = [a - part for a, part in zip(inverse, parts)]
            size *= 2
        solved = [split(dot_full(a, item[2])) for a, item in zip(inverse, items)]
        moved = [fold(mm(item[3], jnp.concatenate(y, axis=1))) for item, y in zip(items, solved)]
        seen = [dot_split(item[1], stack_right(*y)) for item, y in zip(items, solved)]
        for u in range(2):
            p = step * 2 + u
            for half in range(2):
                rest = items[2 * u + half][4] - seen[2 * u + half]
                high = rest.astype(BF16).astype(F32)
                p_ref[p, half * rows : (half + 1) * rows] = jnp.where(
                    first, high, swap(rest - high)
                ).astype(BF16)
            r_ref[:, columns(p)] = jnp.where(first, swap(seen[2 * u]), seen[2 * u + 1])
            z_one, z_two = moved[2 * u][:HD], moved[2 * u + 1][HD:]
            b_ref[p] = jnp.where(first_w, swap(z_one), z_two)
            z = jnp.concatenate([z_one, z_two], axis=0)
            high = z.astype(BF16).astype(F32)
            z_ref[p] = jnp.where(
                lax.broadcasted_iota(jnp.int32, z.shape, 1) < HD, high, swap(z - high)
            ).astype(BF16)

    for ahead in (1, 2):

        @pl.when(me >= ahead)
        def _():
            for which in range(2):
                kv_copy(ahead, which).wait_recv()

    has_far = me >= 2
    has_near = me >= 1

    def attend(p, carry):
        cols = columns(p)
        qf = aq_ref[:, cols].astype(F32) * (1.0 / math.sqrt(HD))
        k_far, k_near, k_own = kbuf[0, :, cols], kbuf[1, :, cols], ak_ref[:, cols]
        v_ends = jnp.concatenate([av_ref[:, cols], vbuf[0, :, cols]], axis=0)
        v_near = vbuf[1, :, cols]
        outs = []
        for half in range(2):
            q = keep(half, qf).astype(BF16)
            far = jnp.where(has_far, mmt(q, k_far), -1e30)
            near = jnp.where(has_near, mmt(q, k_near), -1e30)
            ends = jnp.where(lower, mmt(q, k_own), far)
            largest = jnp.max(jnp.maximum(ends, near), axis=1, keepdims=True)
            e_ends = jnp.exp(ends - largest)
            e_near = jnp.exp(near - largest)
            total = jnp.sum(e_ends + e_near, axis=1, keepdims=True)
            weights = jnp.concatenate(
                [jnp.where(lower, e_ends, 0.0).astype(BF16), jnp.where(lower, 0.0, e_ends).astype(BF16)],
                axis=1,
            )
            outs.append((mm(weights, v_ends) + mm(e_near.astype(BF16), v_near)) / total)
        x = jnp.where(first, outs[0], outs[1])
        att_ref[:, cols] = normed(x) * (ga_ref[:, cols] * 0.5)
        return carry

    def normed(x):
        square = x * x
        mean = jnp.where(first, head_sum(0, square), head_sum(1, square)) * (1.0 / HD)
        return x * lax.rsqrt(mean + 1e-5)

    early = jnp.minimum(jnp.maximum(2 * (me - 6), 0), pairs)
    lax.fori_loop(0, early, attend, 0)

    @pl.loop(0, chunks)
    def _(chunk):
        @pl.when(me > 0)
        def _():
            w_copy(chunk).wait_recv()

        @pl.when(me + 1 < count)
        def _():
            for u in range(CHUNK):
                p = chunk * CHUNK + u
                w = win[p]
                r = fold(mm(z_ref[p], stack_right(*split(w))))
                wout[p] = w - jnp.where(first_w, r[:HD], r[HD:]) + b_ref[p]
            w_copy(chunk).start()

    lax.fori_loop(early, pairs, attend, 0)

    def finish(p, carry):
        cols = columns(p)
        r = fold(mm(p_ref[p], stack_right(*split(win[p]))))
        x = jnp.where(first, r[:rows], r[rows:]) + r_ref[:, cols]
        out_ref[:, cols] = (normed(x) * (gt_ref[:, cols] * 0.5) + att_ref[:, cols]).astype(BF16)
        return carry

    lax.fori_loop(0, pairs, finish, 0)

    @pl.when(me + 1 < count)
    def _():
        @pl.loop(0, chunks)
        def _(chunk):
            w_copy(chunk).wait_send()

    for ahead in (1, 2):

        @pl.when(me + ahead < count)
        def _():
            for which in range(2):
                kv_copy(ahead, which).wait_send()


def per_device(*args):
    (tq, tk, tv, logit, base, init, aq, ak, av, gain_ttt, gain_attn) = args
    rows, width = tq.shape
    pairs = width // PAIR
    chunks = pairs // CHUNK
    count = lax.axis_size("ctx")
    vmem = pl.BlockSpec(memory_space=pltpu.VMEM)
    return pl.pallas_call(
        functools.partial(kernel, count),
        out_shape=jax.ShapeDtypeStruct((rows, width), BF16),
        in_specs=[vmem] * 11,
        out_specs=vmem,
        scratch_shapes=[
            pltpu.VMEM((2, rows, width), BF16),
            pltpu.VMEM((2, rows, width), BF16),
            pltpu.VMEM(logit.shape, F32),
            pltpu.VMEM((pairs, PAIR, PAIR), BF16),
            pltpu.VMEM((pairs, HD, PAIR), F32),
            pltpu.VMEM((pairs, 2 * rows, PAIR), BF16),
            pltpu.VMEM((rows, width), F32),
            pltpu.VMEM((rows, width), F32),
            pltpu.VMEM((pairs, HD, PAIR), F32),
            pltpu.VMEM((pairs, HD, PAIR), F32),
            pltpu.SemaphoreType.DMA((4,)),
            pltpu.SemaphoreType.DMA((4,)),
            pltpu.SemaphoreType.DMA((chunks,)),
            pltpu.SemaphoreType.DMA((chunks,)),
        ],
        compiler_params=pltpu.CompilerParams(
            collective_id=0, has_side_effects=True, vmem_limit_bytes=48 * 1024 * 1024
        ),
    )(tq, tk, tv, logit, base[None], init, aq, ak, av, gain_ttt[None], gain_attn[None])


def solution(mesh):
    split_rows = P(("groups", "ctx"), None)
    in_specs = (split_rows,) * 4 + (P(), P()) + (split_rows,) * 3 + (P(), P())
    return jax.shard_map(
        per_device, mesh=mesh, in_specs=in_specs, out_specs=split_rows, check_vma=False
    )
```

time: 567 us -> 82.9 us (0.15)
  the two profiles are of different devices: /device:TPU:28 before, /device:TPU:29 now
where the time goes in v1:
time: 82.9 us; the launch traced here: 82.4 us
  Pallas kernels  73.2 us (88%)
  local copies, waits for them, and re-layouts  9.12 us (11%)
    pallas_call x1, Pallas kernels, per_device(): pl.pallas_call(functools.partial(kernel, count), out_shape=jax.ShapeDtype...  73.2 us
    unnamed x22, local copies, waits for them, and re-layouts  9.12 us

profile of v1, /device:TPU:29, one launch (start us, length us, event | category | flops | bytes accessed | tf_op | source)
XLA Modules:
  0.0 82.4 jit_solution(5485952035993511586)
XLA Ops:
  0.0 0.0 copy-start.7
  0.0 0.0 copy-start.8
  0.0 0.0 copy-start.9
  0.0 0.9 %copy.12.logit_ref = f32[128,32]{1,0:T(8,128)S(1)} copy(f32[128,32]{0,1:T(8,128)} %param.14) | data formatting | bytes 32768 | tf_op args[3]
  0.9 0.0 copy-done.7
  0.9 0.0 copy-done.8
  0.9 0.0 copy-done.9
  0.9 0.0 copy-start
  0.9 1.2 %copy-done = f32[32,64,64]{2,1,0:T(8,128)S(1)} copy-done((f32[32,64,64]{2,1,0:T(8,128)S(1)}, f32[32,64,64]{2,1,0:T(8,128)}, u32[]{:S(2)}) %copy-start) | copy-done | bytes 524312
  2.1 0.0 copy-start.1
  2.1 1.0 %copy-done.1 = bf16[128,2048]{1,0:T(8,128)(2,1)S(1)} copy-done((bf16[128,2048]{1,0:T(8,128)(2,1)S(1)}, bf16[128,2048]{1,0:T(8,128)(2,1)}, u32[]{:S(2)}) %copy-start.1) | copy-done | bytes 524312
  3.2 0.0 copy-start.2
  3.2 1.0 %copy-done.2 = bf16[128,2048]{1,0:T(8,128)(2,1)S(1)} copy-done((bf16[128,2048]{1,0:T(8,128)(2,1)S(1)}, bf16[128,2048]{1,0:T(8,128)(2,1)}, u32[]{:S(2)}) %copy-start.2) | copy-done | bytes 524312
  4.2 0.0 copy-start.3
  4.2 1.0 %copy-done.3 = bf16[128,2048]{1,0:T(8,128)(2,1)S(1)} copy-done((bf16[128,2048]{1,0:T(8,128)(2,1)S(1)}, bf16[128,2048]{1,0:T(8,128)(2,1)}, u32[]{:S(2)}) %copy-start.3) | copy-done | bytes 524312
  5.2 0.0 copy-start.4
  5.2 1.0 %copy-done.4 = bf16[128,2048]{1,0:T(8,128)(2,1)S(1)} copy-done((bf16[128,2048]{1,0:T(8,128)(2,1)S(1)}, bf16[128,2048]{1,0:T(8,128)(2,1)}, u32[]{:S(2)}) %copy-start.4) | copy-done | bytes 524312
  6.3 0.0 copy-start.5
  6.3 1.0 %copy-done.5 = bf16[128,2048]{1,0:T(8,128)(2,1)S(1)} copy-done((bf16[128,2048]{1,0:T(8,128)(2,1)S(1)}, bf16[128,2048]{1,0:T(8,128)(2,1)}, u32[]{:S(2)}) %copy-start.5) | copy-done | bytes 524312
  7.3 0.0 copy-start.6
  7.3 1.0 %copy-done.6 = bf16[128,2048]{1,0:T(8,128)(2,1)S(1)} copy-done((bf16[128,2048]{1,0:T(8,128)(2,1)S(1)}, bf16[128,2048]{1,0:T(8,128)(2,1)}, u32[]{:S(2)}) %copy-start.6) | copy-done | bytes 524312
  8.4 73.2 %shard_map.109 = bf16[128,2048]{1,0:T(8,128)(2,1)S(1)} custom-call(bf16[128,2048]{1,0:T(8,128)(2,1)S(1)} %copy-done.1, bf16[128,2048]{1,0:T(8,128)(2,1)S(1)} %copy-done.2, bf16[128,2048]{1,0:T(8,128)(2,1)S(1)} %copy-done.3, f32[128,32]{1,0:T(8,128)S(1)} %copy.12.logit_ref, f32[1,32]{1,0:T(1,128)S(1)} %bitcast.5, f32[32,64,64]{2,1,0:T(8,128)S(1)} %copy-done, ...), custom_call_target="tpu_custom_call" | custom-call | tf_op jit(solution)/shard_map/pallas_call | solution.py:315
  81.6 0.8 copy.14
Async XLA Ops:
  0.0 0.9 %copy-start.7 = (f32[2048]{0:T(1024)S(1)}, f32[2048]{0:T(1024)}, u32[]{:S(2)}) copy-start(f32[2048]{0:T(1024)} %param.20) | copy-start | bytes 24580
  0.0 0.9 %copy-start.8 = (f32[2048]{0:T(1024)S(1)}, f32[2048]{0:T(1024)}, u32[]{:S(2)}) copy-start(f32[2048]{0:T(1024)} %param.21) | copy-start | bytes 24580
  0.0 0.9 %copy-start.9 = (f32[32]{0:T(128)S(1)}, f32[32]{0:T(128)}, u32[]{:S(2)}) copy-start(f32[32]{0:T(128)} %param.15) | copy-start | bytes 388
  0.9 1.2 %copy-start = (f32[32,64,64]{2,1,0:T(8,128)S(1)}, f32[32,64,64]{2,1,0:T(8,128)}, u32[]{:S(2)}) copy-start(f32[32,64,64]{2,1,0:T(8,128)} %init_ref.1) | copy-start | bytes 1572868
  2.1 1.0 %copy-start.1 = (bf16[128,2048]{1,0:T(8,128)(2,1)S(1)}, bf16[128,2048]{1,0:T(8,128)(2,1)}, u32[]{:S(2)}) copy-start(bf16[128,2048]{1,0:T(8,128)(2,1)} %tq_ref.1) | copy-start | bytes 1572868
  3.2 1.0 %copy-start.2 = (bf16[128,2048]{1,0:T(8,128)(2,1)S(1)}, bf16[128,2048]{1,0:T(8,128)(2,1)}, u32[]{:S(2)}) copy-start(bf16[128,2048]{1,0:T(8,128)(2,1)} %tk_ref.1) | copy-start | bytes 1572868
  4.2 1.0 %copy-start.3 = (bf16[128,2048]{1,0:T(8,128)(2,1)S(1)}, bf16[128,2048]{1,0:T(8,128)(2,1)}, u32[]{:S(2)}) copy-start(bf16[128,2048]{1,0:T(8,128)(2,1)} %tv_ref.1) | copy-start | bytes 1572868
  5.2 1.0 %copy-start.4 = (bf16[128,2048]{1,0:T(8,128)(2,1)S(1)}, bf16[128,2048]{1,0:T(8,128)(2,1)}, u32[]{:S(2)}) copy-start(bf16[128,2048]{1,0:T(8,128)(2,1)} %aq_ref.1) | copy-start | bytes 1572868
  6.3 1.0 %copy-start.5 = (bf16[128,2048]{1,0:T(8,128)(2,1)S(1)}, bf16[128,2048]{1,0:T(8,128)(2,1)}, u32[]{:S(2)}) copy-start(bf16[128,2048]{1,0:T(8,128)(2,1)} %ak_ref.1) | copy-start | bytes 1572868
  7.3 1.0 %copy-start.6 = (bf16[128,2048]{1,0:T(8,128)(2,1)S(1)}, bf16[128,2048]{1,0:T(8,128)(2,1)}, u32[]{:S(2)}) copy-start(bf16[128,2048]{1,0:T(8,128)(2,1)} %av_ref.1) | copy-start | bytes 1572868

commit v2 on v1

--- a/solution.py
+++ b/solution.py
@@ -60,12 +60,15 @@
     logit_ref,
     base_ref,
     init_ref,
+    aq_hbm,
+    ak_hbm,
+    av_hbm,
+    gt_ref,
+    ga_ref,
+    out_ref,
     aq_ref,
     ak_ref,
     av_ref,
-    gt_ref,
-    ga_ref,
-    out_ref,
     kbuf,
     vbuf,
     eta_ref,
@@ -80,6 +83,7 @@
     kv_recv,
     w_send,
     w_recv,
+    own_sem,
 ):
     rows, width = tq_ref.shape
     pairs = width // PAIR
@@ -87,45 +91,76 @@
     heads = width // HD
     me = lax.axis_index("ctx")
 
+    even = lax.rem(me, 2) == 0
+    odd = jnp.logical_not(even)
+    has_far = me >= 2
+    has_near = me >= 1
+    sends_far = me + 2 < count
+    mirrors = jnp.logical_and(odd, has_far)
+
+    own_copies = [
+        pltpu.make_async_copy(source, target, own_sem.at[at])
+        for at, (source, target) in enumerate(
+            ((aq_hbm, aq_ref), (ak_hbm, ak_ref), (av_hbm, av_ref))
+        )
+    ]
+    for copy in own_copies:
+        copy.start()
+
     barrier = pltpu.get_barrier_semaphore()
-    for back in (1, 2):
-
-        @pl.when(me >= back)
-        def _():
-            pl.semaphore_signal(
-                barrier,
-                inc=1,
-                device_id={"ctx": me - back},
-                device_id_type=pl.DeviceIdType.MESH,
-            )
-
-    @pl.when(me + 1 < count)
-    def _():
-        pl.semaphore_wait(barrier, jnp.minimum(count - 1 - me, 2))
-
-    def kv_copy(ahead, which):
-        source, target = ((ak_ref, kbuf), (av_ref, vbuf))[which]
-        at = 2 * (ahead - 1) + which
+
+    def greet(offset):
+        pl.semaphore_signal(
+            barrier, inc=1, device_id={"ctx": me + offset}, device_id_type=pl.DeviceIdType.MESH
+        )
+
+    pl.when(has_near)(lambda: greet(-1))
+    pl.when(has_far)(lambda: greet(-2))
+    pl.when(jnp.logical_and(even, has_far))(lambda: greet(1))
+    peers = (
+        (me + 1 < count).astype(jnp.int32) + sends_far.astype(jnp.int32) + mirrors.astype(jnp.int32)
+    )
+
+    @pl.when(peers > 0)
+    def _():
+        pl.semaphore_wait(barrier, peers)
+
+    def kv_copy(slot, which, source, target):
+        at = 2 * slot + which
         return pltpu.make_async_remote_copy(
             src_ref=source,
-            dst_ref=target.at[2 - ahead],
+            dst_ref=(kbuf, vbuf)[which].at[slot],
             send_sem=kv_send.at[at],
             recv_sem=kv_recv.at[at],
-            device_id={"ctx": me + ahead},
+            device_id={"ctx": target},
             device_id_type=pl.DeviceIdType.MESH,
         )
 
-    for ahead in (1, 2):
-
-        @pl.when(me + ahead < count)
-        def _():
-            for which in range(2):
-                kv_copy(ahead, which).start()
-
-        @pl.when(me < ahead)
-        def _():
-            kbuf[2 - ahead] = jnp.zeros((rows, width), BF16)
-            vbuf[2 - ahead] = jnp.zeros((rows, width), BF16)
+    def far_copy(which):
+        return kv_copy(0, which, (ak_hbm, av_hbm)[which], me + 2)
+
+    def near_copy(which):
+        return kv_copy(1, which, (ak_hbm, av_hbm)[which], me + 1)
+
+    def mirror_copy(which):
+        return kv_copy(1, which, (kbuf, vbuf)[which].at[0], me - 1)
+
+    @pl.when(sends_far)
+    def _():
+        for which in range(2):
+            far_copy(which).start()
+
+    @pl.when(even)
+    def _():
+        for which in range(2):
+            near_copy(which).start()
+
+    for slot, ready in ((0, has_far), (1, has_near)):
+
+        @pl.when(jnp.logical_not(ready))
+        def _():
+            kbuf[slot] = jnp.zeros((rows, width), BF16)
+            vbuf[slot] = jnp.zeros((rows, width), BF16)
 
     def w_copy(chunk):
         span = pl.ds(chunk * CHUNK, CHUNK)
@@ -222,15 +257,24 @@
                 lax.broadcasted_iota(jnp.int32, z.shape, 1) < HD, high, swap(z - high)
             ).astype(BF16)
 
-    for ahead in (1, 2):
-
-        @pl.when(me >= ahead)
+    def take_window():
+        @pl.when(has_far)
         def _():
             for which in range(2):
-                kv_copy(ahead, which).wait_recv()
-
-    has_far = me >= 2
-    has_near = me >= 1
+                far_copy(which).wait_recv()
+
+        @pl.when(mirrors)
+        def _():
+            for which in range(2):
+                mirror_copy(which).start()
+
+        @pl.when(has_near)
+        def _():
+            for which in range(2):
+                near_copy(which).wait_recv()
+
+    for copy in own_copies:
+        copy.wait()
 
     def attend(p, carry):
         cols = columns(p)
@@ -262,7 +306,9 @@
         mean = jnp.where(first, head_sum(0, square), head_sum(1, square)) * (1.0 / HD)
         return x * lax.rsqrt(mean + 1e-5)
 
-    early = jnp.minimum(jnp.maximum(2 * (me - 6), 0), pairs)
+    window_first = me >= 11
+    early = jnp.where(window_first, jnp.minimum(2 * (me - 11), pairs // 2), 0)
+    pl.when(window_first)(take_window)
     lax.fori_loop(0, early, attend, 0)
 
     @pl.loop(0, chunks)
@@ -280,6 +326,7 @@
                 wout[p] = w - jnp.where(first_w, r[:HD], r[HD:]) + b_ref[p]
             w_copy(chunk).start()
 
+    pl.when(jnp.logical_not(window_first))(take_window)
     lax.fori_loop(early, pairs, attend, 0)
 
     def finish(p, carry):
@@ -297,12 +344,20 @@
         def _(chunk):
             w_copy(chunk).wait_send()
 
-    for ahead in (1, 2):
-
-        @pl.when(me + ahead < count)
-        def _():
-            for which in range(2):
-                kv_copy(ahead, which).wait_send()
+    @pl.when(sends_far)
+    def _():
+        for which in range(2):
+            far_copy(which).wait_send()
+
+    @pl.when(even)
+    def _():
+        for which in range(2):
+            near_copy(which).wait_send()
+
+    @pl.when(mirrors)
+    def _():
+        for which in range(2):
+            mirror_copy(which).wait_send()
 
 
 def per_device(*args):
@@ -312,12 +367,16 @@
     chunks = pairs // CHUNK
     count = lax.axis_size("ctx")
     vmem = pl.BlockSpec(memory_space=pltpu.VMEM)
+    hbm = pl.BlockSpec(memory_space=pltpu.HBM)
     return pl.pallas_call(
         functools.partial(kernel, count),
         out_shape=jax.ShapeDtypeStruct((rows, width), BF16),
-        in_specs=[vmem] * 11,
+        in_specs=[vmem] * 6 + [hbm] * 3 + [vmem] * 2,
         out_specs=vmem,
         scratch_shapes=[
+            pltpu.VMEM((rows, width), BF16),
+            pltpu.VMEM((rows, width), BF16),
+            pltpu.VMEM((rows, width), BF16),
             pltpu.VMEM((2, rows, width), BF16),
             pltpu.VMEM((2, rows, width), BF16),
             pltpu.VMEM(logit.shape, F32),
@@ -332,6 +391,7 @@
             pltpu.SemaphoreType.DMA((4,)),
             pltpu.SemaphoreType.DMA((chunks,)),
             pltpu.SemaphoreType.DMA((chunks,)),
+            pltpu.SemaphoreType.DMA((3,)),
         ],
         compiler_params=pltpu.CompilerParams(
             collective_id=0, has_side_effects=True, vmem_limit_bytes=48 * 1024 * 1024

time: 82.9 us -> 78.4 us (0.946)
  the two profiles are of different devices: /device:TPU:29 before, /device:TPU:28 now
where the time goes in v2:
time: 78.4 us; the launch traced here: 77.9 us
  Pallas kernels  68.7 us (88%)
  local copies, waits for them, and re-layouts  9.12 us (12%)
    pallas_call x1, Pallas kernels, per_device(): pl.pallas_call(functools.partial(kernel, count), out_shape=jax.ShapeDtype...  68.7 us
    unnamed x22, local copies, waits for them, and re-layouts  9.12 us

profile of v2, /device:TPU:28, one launch (start us, length us, event | category | flops | bytes accessed | tf_op | source)
XLA Modules:
  0.0 77.9 jit_solution(13498394553042393928)
XLA Ops:
  0.0 0.0 copy-start.7
  0.0 0.0 copy-start.8
  0.0 0.0 copy-start.9
  0.0 0.9 %copy.12.logit_ref = f32[128,32]{1,0:T(8,128)S(1)} copy(f32[128,32]{0,1:T(8,128)} %param.14) | data formatting | bytes 32768 | tf_op args[3]
  0.9 0.0 copy-done.7
  0.9 0.0 copy-done.8
  0.9 0.0 copy-done.9
  0.9 0.0 copy-start
  0.9 1.2 %copy-done = f32[32,64,64]{2,1,0:T(8,128)S(1)} copy-done((f32[32,64,64]{2,1,0:T(8,128)S(1)}, f32[32,64,64]{2,1,0:T(8,128)}, u32[]{:S(2)}) %copy-start) | copy-done | bytes 524312
  2.1 0.0 copy-start.1
  2.1 1.0 %copy-done.1 = bf16[128,2048]{1,0:T(8,128)(2,1)S(1)} copy-done((bf16[128,2048]{1,0:T(8,128)(2,1)S(1)}, bf16[128,2048]{1,0:T(8,128)(2,1)}, u32[]{:S(2)}) %copy-start.1) | copy-done | bytes 524312
  3.2 0.0 copy-start.2
  3.2 1.0 %copy-done.2 = bf16[128,2048]{1,0:T(8,128)(2,1)S(1)} copy-done((bf16[128,2048]{1,0:T(8,128)(2,1)S(1)}, bf16[128,2048]{1,0:T(8,128)(2,1)}, u32[]{:S(2)}) %copy-start.2) | copy-done | bytes 524312
  4.2 0.0 copy-start.3
  4.2 1.0 %copy-done.3 = bf16[128,2048]{1,0:T(8,128)(2,1)S(1)} copy-done((bf16[128,2048]{1,0:T(8,128)(2,1)S(1)}, bf16[128,2048]{1,0:T(8,128)(2,1)}, u32[]{:S(2)}) %copy-start.3) | copy-done | bytes 524312
  5.2 0.0 copy-start.4
  5.2 1.0 %copy-done.4 = bf16[128,2048]{1,0:T(8,128)(2,1)S(1)} copy-done((bf16[128,2048]{1,0:T(8,128)(2,1)S(1)}, bf16[128,2048]{1,0:T(8,128)(2,1)}, u32[]{:S(2)}) %copy-start.4) | copy-done | bytes 524312
  6.3 0.0 copy-start.5
  6.3 1.0 %copy-done.5 = bf16[128,2048]{1,0:T(8,128)(2,1)S(1)} copy-done((bf16[128,2048]{1,0:T(8,128)(2,1)S(1)}, bf16[128,2048]{1,0:T(8,128)(2,1)}, u32[]{:S(2)}) %copy-start.5) | copy-done | bytes 524312
  7.3 0.0 copy-start.6
  7.3 1.0 %copy-done.6 = bf16[128,2048]{1,0:T(8,128)(2,1)S(1)} copy-done((bf16[128,2048]{1,0:T(8,128)(2,1)S(1)}, bf16[128,2048]{1,0:T(8,128)(2,1)}, u32[]{:S(2)}) %copy-start.6) | copy-done | bytes 524312
  8.4 68.7 %shard_map.109 = bf16[128,2048]{1,0:T(8,128)(2,1)S(1)} custom-call(bf16[128,2048]{1,0:T(8,128)(2,1)S(1)} %copy-done.1, bf16[128,2048]{1,0:T(8,128)(2,1)S(1)} %copy-done.2, bf16[128,2048]{1,0:T(8,128)(2,1)S(1)} %copy-done.3, f32[128,32]{1,0:T(8,128)S(1)} %copy.12.logit_ref, f32[1,32]{1,0:T(1,128)S(1)} %bitcast.5, f32[32,64,64]{2,1,0:T(8,128)S(1)} %copy-done, ...), custom_call_target="tpu_custom_call" | custom-call | tf_op jit(solution)/shard_map/pallas_call | solution.py:371
  77.1 0.8 %copy.14 = bf16[128,2048]{1,0:T(8,128)(2,1)} copy(bf16[128,2048]{1,0:T(8,128)(2,1)S(1)} %shard_map.109) | data formatting | bytes 1048576
Async XLA Ops:
  0.0 0.9 %copy-start.7 = (f32[2048]{0:T(1024)S(1)}, f32[2048]{0:T(1024)}, u32[]{:S(2)}) copy-start(f32[2048]{0:T(1024)} %param.20) | copy-start | bytes 24580
  0.0 0.9 %copy-start.8 = (f32[2048]{0:T(1024)S(1)}, f32[2048]{0:T(1024)}, u32[]{:S(2)}) copy-start(f32[2048]{0:T(1024)} %param.21) | copy-start | bytes 24580
  0.0 0.9 %copy-start.9 = (f32[32]{0:T(128)S(1)}, f32[32]{0:T(128)}, u32[]{:S(2)}) copy-start(f32[32]{0:T(128)} %param.15) | copy-start | bytes 388
  0.9 1.2 %copy-start = (f32[32,64,64]{2,1,0:T(8,128)S(1)}, f32[32,64,64]{2,1,0:T(8,128)}, u32[]{:S(2)}) copy-start(f32[32,64,64]{2,1,0:T(8,128)} %init_ref.1) | copy-start | bytes 1572868
  2.1 1.0 %copy-start.1 = (bf16[128,2048]{1,0:T(8,128)(2,1)S(1)}, bf16[128,2048]{1,0:T(8,128)(2,1)}, u32[]{:S(2)}) copy-start(bf16[128,2048]{1,0:T(8,128)(2,1)} %tq_ref.1) | copy-start | bytes 1572868
  3.2 1.0 %copy-start.2 = (bf16[128,2048]{1,0:T(8,128)(2,1)S(1)}, bf16[128,2048]{1,0:T(8,128)(2,1)}, u32[]{:S(2)}) copy-start(bf16[128,2048]{1,0:T(8,128)(2,1)} %tk_ref.1) | copy-start | bytes 1572868
  4.2 1.0 %copy-start.3 = (bf16[128,2048]{1,0:T(8,128)(2,1)S(1)}, bf16[128,2048]{1,0:T(8,128)(2,1)}, u32[]{:S(2)}) copy-start(bf16[128,2048]{1,0:T(8,128)(2,1)} %tv_ref.1) | copy-start | bytes 1572868
  5.2 1.0 %copy-start.4 = (bf16[128,2048]{1,0:T(8,128)(2,1)S(1)}, bf16[128,2048]{1,0:T(8,128)(2,1)}, u32[]{:S(2)}) copy-start(bf16[128,2048]{1,0:T(8,128)(2,1)} %aq_hbm.1) | copy-start | bytes 1572868
  6.3 1.0 %copy-start.5 = (bf16[128,2048]{1,0:T(8,128)(2,1)S(1)}, bf16[128,2048]{1,0:T(8,128)(2,1)}, u32[]{:S(2)}) copy-start(bf16[128,2048]{1,0:T(8,128)(2,1)} %ak_hbm.1) | copy-start | bytes 1572868
  7.3 1.0 %copy-start.6 = (bf16[128,2048]{1,0:T(8,128)(2,1)S(1)}, bf16[128,2048]{1,0:T(8,128)(2,1)}, u32[]{:S(2)}) copy-start(bf16[128,2048]{1,0:T(8,128)(2,1)} %av_hbm.1) | copy-start | bytes 1572868

commit v3 on v2

--- a/solution.py
+++ b/solution.py
@@ -125,34 +125,36 @@
     def _():
         pl.semaphore_wait(barrier, peers)
 
-    def kv_copy(slot, which, source, target):
-        at = 2 * slot + which
+    def kv_copy(slot, item, source, target):
+        which, part = item % 2, item // 2
+        at = 4 * slot + item
+        span = pl.ds(part * (width // 2), width // 2)
         return pltpu.make_async_remote_copy(
-            src_ref=source,
-            dst_ref=(kbuf, vbuf)[which].at[slot],
+            src_ref=source.at[:, span],
+            dst_ref=(kbuf, vbuf)[which].at[slot, :, span],
             send_sem=kv_send.at[at],
             recv_sem=kv_recv.at[at],
             device_id={"ctx": target},
             device_id_type=pl.DeviceIdType.MESH,
         )
 
-    def far_copy(which):
-        return kv_copy(0, which, (ak_hbm, av_hbm)[which], me + 2)
-
-    def near_copy(which):
-        return kv_copy(1, which, (ak_hbm, av_hbm)[which], me + 1)
-
-    def mirror_copy(which):
-        return kv_copy(1, which, (kbuf, vbuf)[which].at[0], me - 1)
+    def far_copy(item):
+        return kv_copy(0, item, (ak_hbm, av_hbm)[item % 2], me + 2)
+
+    def near_copy(item):
+        return kv_copy(1, item, (ak_hbm, av_hbm)[item % 2], me + 1)
+
+    def mirror_copy(item):
+        return kv_copy(1, item, (kbuf, vbuf)[item % 2].at[0], me - 1)
 
     @pl.when(sends_far)
     def _():
-        for which in range(2):
+        for which in range(4):
             far_copy(which).start()
 
     @pl.when(even)
     def _():
-        for which in range(2):
+        for which in range(4):
             near_copy(which).start()
 
     for slot, ready in ((0, has_far), (1, has_near)):
@@ -257,20 +259,20 @@
                 lax.broadcasted_iota(jnp.int32, z.shape, 1) < HD, high, swap(z - high)
             ).astype(BF16)
 
-    def take_window():
+    def take_window(part):
         @pl.when(has_far)
         def _():
-            for which in range(2):
+            for which in (2 * part, 2 * part + 1):
                 far_copy(which).wait_recv()
 
         @pl.when(mirrors)
         def _():
-            for which in range(2):
+            for which in (2 * part, 2 * part + 1):
                 mirror_copy(which).start()
 
         @pl.when(has_near)
         def _():
-            for which in range(2):
+            for which in (2 * part, 2 * part + 1):
                 near_copy(which).wait_recv()
 
     for copy in own_copies:
@@ -308,7 +310,7 @@
 
     window_first = me >= 11
     early = jnp.where(window_first, jnp.minimum(2 * (me - 11), pairs // 2), 0)
-    pl.when(window_first)(take_window)
+    pl.when(window_first)(lambda: take_window(0))
     lax.fori_loop(0, early, attend, 0)
 
     @pl.loop(0, chunks)
@@ -326,8 +328,10 @@
                 wout[p] = w - jnp.where(first_w, r[:HD], r[HD:]) + b_ref[p]
             w_copy(chunk).start()
 
-    pl.when(jnp.logical_not(window_first))(take_window)
-    lax.fori_loop(early, pairs, attend, 0)
+    pl.when(jnp.logical_not(window_first))(lambda: take_window(0))
+    lax.fori_loop(early, pairs // 2, attend, 0)
+    take_window(1)
+    lax.fori_loop(pairs // 2, pairs, attend, 0)
 
     def finish(p, carry):
         cols = columns(p)
@@ -346,17 +350,17 @@
 
     @pl.when(sends_far)
     def _():
-        for which in range(2):
+        for which in range(4):
             far_copy(which).wait_send()
 
     @pl.when(even)
     def _():
-        for which in range(2):
+        for which in range(4):
             near_copy(which).wait_send()
 
     @pl.when(mirrors)
     def _():
-        for which in range(2):
+        for which in range(4):
             mirror_copy(which).wait_send()
 
 
@@ -387,8 +391,8 @@
             pltpu.VMEM((rows, width), F32),
             pltpu.VMEM((pairs, HD, PAIR), F32),
             pltpu.VMEM((pairs, HD, PAIR), F32),
-            pltpu.SemaphoreType.DMA((4,)),
-            pltpu.SemaphoreType.DMA((4,)),
+            pltpu.SemaphoreType.DMA((8,)),
+            pltpu.SemaphoreType.DMA((8,)),
             pltpu.SemaphoreType.DMA((chunks,)),
             pltpu.SemaphoreType.DMA((chunks,)),
             pltpu.SemaphoreType.DMA((3,)),

time: 78.4 us -> 79.5 us (1.014)
  Pallas kernels: 68.7 us -> 69.9 us
    pallas_call x1, Pallas kernels: 68.7 us -> 69.9 us  [per_device(): pl.pallas_call(functools.partial(kernel, count), out_shape=jax.ShapeDtype...]
where the time goes in v3:
time: 79.5 us; the launch traced here: 79 us
  Pallas kernels  69.9 us (88%)
  local copies, waits for them, and re-layouts  9.12 us (11%)
    pallas_call x1, Pallas kernels, per_device(): pl.pallas_call(functools.partial(kernel, count), out_shape=jax.ShapeDtype...  69.9 us
    unnamed x22, local copies, waits for them, and re-layouts  9.12 us

profile of v3, /device:TPU:28, one launch (start us, length us, event | category | flops | bytes accessed | tf_op | source)
XLA Modules:
  0.0 79.0 jit_solution(14061509310979913853)
XLA Ops:
  0.0 0.0 copy-start.7
  0.0 0.0 copy-start.8
  0.0 0.0 copy-start.9
  0.0 0.9 %copy.12.logit_ref = f32[128,32]{1,0:T(8,128)S(1)} copy(f32[128,32]{0,1:T(8,128)} %param.14) | data formatting | bytes 32768 | tf_op args[3]
  0.9 0.0 copy-done.7
  0.9 0.0 copy-done.8
  0.9 0.0 copy-done.9
  0.9 0.0 copy-start
  0.9 1.2 %copy-done = f32[32,64,64]{2,1,0:T(8,128)S(1)} copy-done((f32[32,64,64]{2,1,0:T(8,128)S(1)}, f32[32,64,64]{2,1,0:T(8,128)}, u32[]{:S(2)}) %copy-start) | copy-done | bytes 524312
  2.1 0.0 copy-start.1
  2.1 1.0 %copy-done.1 = bf16[128,2048]{1,0:T(8,128)(2,1)S(1)} copy-done((bf16[128,2048]{1,0:T(8,128)(2,1)S(1)}, bf16[128,2048]{1,0:T(8,128)(2,1)}, u32[]{:S(2)}) %copy-start.1) | copy-done | bytes 524312
  3.2 0.0 copy-start.2
  3.2 1.0 %copy-done.2 = bf16[128,2048]{1,0:T(8,128)(2,1)S(1)} copy-done((bf16[128,2048]{1,0:T(8,128)(2,1)S(1)}, bf16[128,2048]{1,0:T(8,128)(2,1)}, u32[]{:S(2)}) %copy-start.2) | copy-done | bytes 524312
  4.2 0.0 copy-start.3
  4.2 1.0 %copy-done.3 = bf16[128,2048]{1,0:T(8,128)(2,1)S(1)} copy-done((bf16[128,2048]{1,0:T(8,128)(2,1)S(1)}, bf16[128,2048]{1,0:T(8,128)(2,1)}, u32[]{:S(2)}) %copy-start.3) | copy-done | bytes 524312
  5.2 0.0 copy-start.4
  5.2 1.0 %copy-done.4 = bf16[128,2048]{1,0:T(8,128)(2,1)S(1)} copy-done((bf16[128,2048]{1,0:T(8,128)(2,1)S(1)}, bf16[128,2048]{1,0:T(8,128)(2,1)}, u32[]{:S(2)}) %copy-start.4) | copy-done | bytes 524312
  6.3 0.0 copy-start.5
  6.3 1.0 %copy-done.5 = bf16[128,2048]{1,0:T(8,128)(2,1)S(1)} copy-done((bf16[128,2048]{1,0:T(8,128)(2,1)S(1)}, bf16[128,2048]{1,0:T(8,128)(2,1)}, u32[]{:S(2)}) %copy-start.5) | copy-done | bytes 524312
  7.3 0.0 copy-start.6
  7.3 1.0 %copy-done.6 = bf16[128,2048]{1,0:T(8,128)(2,1)S(1)} copy-done((bf16[128,2048]{1,0:T(8,128)(2,1)S(1)}, bf16[128,2048]{1,0:T(8,128)(2,1)}, u32[]{:S(2)}) %copy-start.6) | copy-done | bytes 524312
  8.4 69.9 %shard_map.109 = bf16[128,2048]{1,0:T(8,128)(2,1)S(1)} custom-call(bf16[128,2048]{1,0:T(8,128)(2,1)S(1)} %copy-done.1, bf16[128,2048]{1,0:T(8,128)(2,1)S(1)} %copy-done.2, bf16[128,2048]{1,0:T(8,128)(2,1)S(1)} %copy-done.3, f32[128,32]{1,0:T(8,128)S(1)} %copy.12.logit_ref, f32[1,32]{1,0:T(1,128)S(1)} %bitcast.5, f32[32,64,64]{2,1,0:T(8,128)S(1)} %copy-done, ...), custom_call_target="tpu_custom_call" | custom-call | tf_op jit(solution)/shard_map/pallas_call | solution.py:375
  78.2 0.8 %copy.14 = bf16[128,2048]{1,0:T(8,128)(2,1)} copy(bf16[128,2048]{1,0:T(8,128)(2,1)S(1)} %shard_map.109) | data formatting | bytes 1048576
Async XLA Ops:
  0.0 0.9 %copy-start.7 = (f32[2048]{0:T(1024)S(1)}, f32[2048]{0:T(1024)}, u32[]{:S(2)}) copy-start(f32[2048]{0:T(1024)} %param.20) | copy-start | bytes 24580
  0.0 0.9 %copy-start.8 = (f32[2048]{0:T(1024)S(1)}, f32[2048]{0:T(1024)}, u32[]{:S(2)}) copy-start(f32[2048]{0:T(1024)} %param.21) | copy-start | bytes 24580
  0.0 0.9 %copy-start.9 = (f32[32]{0:T(128)S(1)}, f32[32]{0:T(128)}, u32[]{:S(2)}) copy-start(f32[32]{0:T(128)} %param.15) | copy-start | bytes 388
  0.9 1.2 %copy-start = (f32[32,64,64]{2,1,0:T(8,128)S(1)}, f32[32,64,64]{2,1,0:T(8,128)}, u32[]{:S(2)}) copy-start(f32[32,64,64]{2,1,0:T(8,128)} %init_ref.1) | copy-start | bytes 1572868
  2.1 1.0 %copy-start.1 = (bf16[128,2048]{1,0:T(8,128)(2,1)S(1)}, bf16[128,2048]{1,0:T(8,128)(2,1)}, u32[]{:S(2)}) copy-start(bf16[128,2048]{1,0:T(8,128)(2,1)} %tq_ref.1) | copy-start | bytes 1572868
  3.2 1.0 %copy-start.2 = (bf16[128,2048]{1,0:T(8,128)(2,1)S(1)}, bf16[128,2048]{1,0:T(8,128)(2,1)}, u32[]{:S(2)}) copy-start(bf16[128,2048]{1,0:T(8,128)(2,1)} %tk_ref.1) | copy-start | bytes 1572868
  4.2 1.0 %copy-start.3 = (bf16[128,2048]{1,0:T(8,128)(2,1)S(1)}, bf16[128,2048]{1,0:T(8,128)(2,1)}, u32[]{:S(2)}) copy-start(bf16[128,2048]{1,0:T(8,128)(2,1)} %tv_ref.1) | copy-start | bytes 1572868
  5.2 1.0 %copy-start.4 = (bf16[128,2048]{1,0:T(8,128)(2,1)S(1)}, bf16[128,2048]{1,0:T(8,128)(2,1)}, u32[]{:S(2)}) copy-start(bf16[128,2048]{1,0:T(8,128)(2,1)} %aq_hbm.1) | copy-start | bytes 1572868
  6.3 1.0 %copy-start.5 = (bf16[128,2048]{1,0:T(8,128)(2,1)S(1)}, bf16[128,2048]{1,0:T(8,128)(2,1)}, u32[]{:S(2)}) copy-start(bf16[128,2048]{1,0:T(8,128)(2,1)} %ak_hbm.1) | copy-start | bytes 1572868
  7.3 1.0 %copy-start.6 = (bf16[128,2048]{1,0:T(8,128)(2,1)S(1)}, bf16[128,2048]{1,0:T(8,128)(2,1)}, u32[]{:S(2)}) copy-start(bf16[128,2048]{1,0:T(8,128)(2,1)} %av_hbm.1) | copy-start | bytes 1572868
